TPU v7x, 32 devices: a whole 2x2x4 slice. The times are simulated.
32 devices in a mesh: row: 4 (over x, core), col: 8 (over z, y).
Axes of the slice: x: 2, y: 2, z: 4, core: 2. Of those that a mesh axis runs over, the one named last changes fastest.
Arguments:
- features: bfloat16 [2048, 256], P(('row', 'col')), may hold values from -6 to 6
- adj_tiles: bfloat16 [4, 8, 3, 128, 128], P('row', 'col'), may hold values from -0.3125 to 0.3125
- tile_coord: int32 [4, 8, 3], P('row', 'col'), may hold values from 0 to 7, as said below
- tile_count: int32 [4, 8], P('row', 'col'), may hold values from 1 to 3, as said below
- weight: bfloat16 [256, 256], replicated, may hold values from -0.375 to 0.375
Outputs:
- out: bfloat16 [2048, 256], P(('col', 'row'))
Inputs may be any that keep to these rules, and one draw needn't show every extreme that they name: `tile_coord`: each entry is t * 4 + s for a target tile t and a source tile s; within one device's list all entries differ. `tile_count`: slots from this number on are not part of the adjacency.
All inputs are finite; a program needn't handle non-finite values.
Results may differ from a plain program's by a relative error of at most 0.0049.
Values may be sent and summed in bfloat16 or wider, within the bound.
A program may use at most 128 MiB of HBM per device.

v0:
```python
import math

import jax
import jax.numpy as jnp
from jax import lax
from jax.sharding import PartitionSpec as P


def on_device(features, adj_tiles, tile_coord, tile_count, weight):
    tile_size = adj_tiles.shape[-1]
    feat_width = features.shape[1]
    slot_count = adj_tiles.shape[2]
    local_rows = features.shape[0]
    target_count = local_rows * lax.axis_size("row") // tile_size
    source_count = local_rows * lax.axis_size("col") // tile_size
    tile_vals = adj_tiles[0, 0]
    coord_list = tile_coord[0, 0]
    live_slot = jnp.arange(slot_count) < tile_count[0, 0]
    tile_vals = jnp.where(live_slot[:, None, None], tile_vals, jnp.zeros_like(tile_vals))
    target = coord_list // source_count
    source = coord_list % source_count
    gathered = lax.all_gather(features, "col", axis=0, tiled=True)
    source_tiles = gathered.reshape(source_count, tile_size, feat_width)
    group_size = math.gcd(slot_count, 16)
    steps_count = slot_count // group_size
    inputs = (
        tile_vals.reshape(steps_count, group_size, tile_size, tile_size),
        source.reshape(steps_count, group_size),
        target.reshape(steps_count, group_size),
    )

    def add_group(total, items):
        tile_group, src_group, target_group = items
        feat_rows = source_tiles[src_group]
        products = jnp.einsum(
            "kij,kjf->kif", tile_group, feat_rows, preferred_element_type=jnp.float32
        )
        total = total.at[target_group].add(products)
        return (total, None)

    start_total = jnp.zeros((target_count, tile_size, feat_width), jnp.float32)
    total, unused = lax.scan(add_group, start_total, inputs)
    partial_value = total.reshape(target_count * tile_size, feat_width)
    hidden = lax.psum_scatter(partial_value, "row", scatter_dimension=0, tiled=True).astype(
        jnp.bfloat16
    )
    mixed = jnp.dot(hidden, weight, preferred_element_type=jnp.float32)
    return jax.nn.relu(mixed).astype(jnp.bfloat16)


def solution(mesh):
    return jax.shard_map(
        on_device,
        mesh=mesh,
        in_specs=(
            P(("row", "col"), None),
            P("row", "col", None, None, None),
            P("row", "col", None),
            P("row", "col"),
            P(),
        ),
        out_specs=P(("col", "row"), None),
        check_vma=False,
    )
```

profile of v0, /device:TPU:0, one launch (start us, length us, event | category | flops | bytes accessed | tf_op | source)
XLA Modules:
  0.0 90.0 jit_solution(17176452782541059032)
XLA Ops:
  6.5 0.0 copy-start
  6.5 0.0 reduce-scatter.2.cloned.1.call-start
  6.5 0.7 and_select_fusion
  7.2 0.0 copy-start.2
  7.2 32.9 %all_gather.3 = bf16[512,256]{1,0:T(8,128)(2,1)S(1)} all-gather(bf16[64,256]{1,0:T(8,128)(2,1)} %param.9), channel_id=1, replica_groups=mesh['row'=4,'col'=8] {'col'}, dimensions={0}, use_global_device_ids=true | all-gather | bytes 294912 | tf_op jit(solution)/shard_map/all_gather | solution.py:22
  40.8 0.0 copy-done.2
  40.8 0.1 bitcast_select_fusion
  40.9 0.0 copy-start.3
  40.9 0.6 copy-done.3
  41.5 18.1 %while.12 = (s32[]{:T(128)}, f32[2,128,256]{2,1,0:T(8,128)S(1)}, s32[3,1]{0,1:T(1,128)S(1)}, bf16[3,1,128,128]{3,2,1,0:T(8,128)(2,1)S(1)}, s32[3,1]{0,1:T(1,128)...) while((s32[]{:T(128)}, f32[2,128,256]{2,1,0:T(8,128)S(1)}, ...), condition=%wide.region_2.3_spmd, body=%wide.region_0.2_spmd.sunk | while | flops 8454169 | bytes 360679 | solution.py:42
  41.5 0.7 constant_dynamic-slice_fusion.3
  44.3 0.7 and_reduce_fusion.2
  46.8 0.7 fusion.16
  47.6 0.7 constant_dynamic-slice_fusion.3
  50.3 0.7 and_reduce_fusion.2
  52.9 0.7 fusion.16
  53.6 0.7 constant_dynamic-slice_fusion.3
  56.3 0.7 and_reduce_fusion.2
  58.9 0.7 fusion.16
  59.6 0.0 copy-start.1
  59.6 0.7 copy-done.1
  60.3 0.0 reduce-scatter.2.cloned.1.call-update
  60.4 21.2 %reduce-scatter.2.cloned.1.call-done = f32[64,256]{1,0:T(8,128)} async-done(((f32[256,256]{1,0:T(8,128)}), f32[64,256]{1,0:T(8,128)}) %reduce-scatter.2.cloned.1.call-update) | async-done | bytes 65552 | tf_op jit(solution)/shard_map/reduce_scatter | solution.py:44
  81.5 0.0 copy-done
  81.5 1.6 %fusion.8 = bf16[64,256]{1,0:T(8,128)(2,1)} fusion(bf16[256,256]{1,0:T(8,128)(2,1)S(1)} %copy-done, f32[64,256]{1,0:T(8,128)} %reduce-scatter.2.cloned.1.call-done), kind=kOutput, calls=%fused_computation.13 | convolution fusion | flops 8437760 | bytes 229376 | tf_op jit(solution)/shard_map/dot_general | solution.py:47
  (2 shorter events, 0.0 us)
Async XLA Ops:
  6.5 75.0 %copy-start = (bf16[256,256]{1,0:T(8,128)(2,1)S(1)}, bf16[256,256]{1,0:T(8,128)(2,1)}, u32[]{:S(2)}) copy-start(bf16[256,256]{1,0:T(8,128)(2,1)} %param.13) | copy-start | bytes 393220
  6.5 75.0 %reduce-scatter.2.cloned.1.call-start = ((), (), s32[]{:S(2)}) async-start(), calls=%async_computation.1 | async-start | bytes 327680 | tf_op jit(solution)/shard_map/reduce_scatter | solution.py:44
  7.2 33.5 %copy-start.2 = (bf16[1,1,3,128,128]{4,3,2,1,0:T(8,128)(2,1)S(1)}, bf16[1,1,3,128,128]{4,3,2,1,0:T(8,128)(2,1)}, u32[]{:S(2)}) copy-start(bf16[1,1,3,128,128]{4,3,2,1,0:T(8,128)(2,1)} %param.10) | copy-start | bytes 294916
  40.9 0.7 copy-start.3
  59.6 0.7 copy-start.1
Sparse Core Ops, SparseCore 0:
  60.5 21.0 reduce-scatter.1
where the time goes:
time: 90.4 us; the launch traced here: 90 us
  blocking collectives  32.9 us (36%)
  waiting for transfers between devices  21.2 us (23%)
  between operations  14.1 us (16%)
  loops' own time  11.8 us (13%)
  matrix products  3.75 us (4%)
  local copies, waits for them, and re-layouts  3.34 us (4%)
  other arithmetic  2.9 us (3%)
    all_gather x1, blocking collectives, on_device(): gathered = lax.all_gather(features, 'col', axis=0, tiled=True)  32.9 us
    reduce_scatter x1, waiting for transfers between devices, on_device(): lax.psum_scatter(partial_value, 'row', scatter_dimension=0, tiled=True)  21.2 us
    another operation x1, loops' own time, on_device(): total, unused = lax.scan(add_group, start_total, inputs)  11.8 us
    dot_general x3, matrix products, add_group(): jnp.einsum('kij,kjf->kif', tile_group, feat_rows, preferred_element_type=...  2.14 us
    another operation x3, other arithmetic  2.11 us
    dynamic_slice x3, local copies, waits for them, and re-layouts, on_device(): total, unused = lax.scan(add_group, start_total, inputs)  2 us
  transfers between devices with their start and end apart: 1, of which 1 were waited for; matrix products, arithmetic and copies ran while one was open for 0% of the time, Pallas kernels for 0%

commit v1 on v0

v1 whole, which is shorter than its diff:
```python
import functools

import jax
import jax.numpy as jnp
from jax import lax
from jax.experimental import pallas as pl
from jax.experimental.pallas import tpu as pltpu
from jax.sharding import PartitionSpec as P

MESH = pl.DeviceIdType.MESH
F32 = jnp.float32
BF16 = jnp.bfloat16


def kernel(
    n_row, n_z, n_y,
    x_ref, adj_ref, coord_ref, count_ref, w_ref, out_ref,
    feats, adj, weight, dense, total, stage, parts,
    own_sem, adj_sem, weight_sem, z_send, z_recv, y_send, y_recv, row_send, row_recv,
):
    row, col = lax.axis_index("row"), lax.axis_index("col")
    z, y = col // n_y, col % n_y
    slots, tile = adj_ref.shape[2], adj_ref.shape[3]
    rows = x_ref.shape[0]
    n_tgt = n_row * rows // tile
    n_src = n_z * n_y * rows // tile

    def piece(z_at, y_at):
        return feats.at[pl.ds(pl.multiple_of((z_at * n_y + y_at) * rows, rows), rows)]

    def z_peer(d):
        return {"col": lax.rem(z + d, n_z) * n_y + y}

    def y_peer(e):
        return {"col": z * n_y + lax.rem(y + e, n_y)}

    def row_peer(d):
        return {"row": lax.rem(row + d, n_row)}

    def back(at, d, n):
        return lax.rem(at + n - d, n)

    own_copy = pltpu.make_async_copy(x_ref, piece(z, y), own_sem)
    own_copy.start()
    adj_copy = pltpu.make_async_copy(adj_ref.at[0, 0], adj, adj_sem)
    adj_copy.start()
    weight_copy = pltpu.make_async_copy(w_ref, weight, weight_sem)
    weight_copy.start()

    barrier = pltpu.get_barrier_semaphore()
    peers = [z_peer(d) for d in range(1, n_z)]
    peers += [y_peer(e) for e in range(1, n_y)]
    peers += [row_peer(d) for d in range(1, n_row)]
    for peer in peers:
        pl.semaphore_signal(barrier, inc=1, device_id=peer, device_id_type=MESH)
    pl.semaphore_wait(barrier, len(peers))
    own_copy.wait()

    def z_copy(d, block):
        return pltpu.make_async_remote_copy(
            src_ref=block, dst_ref=block, send_sem=z_send.at[d], recv_sem=z_recv.at[d],
            device_id=z_peer(d), device_id_type=MESH,
        )

    def y_copy(e, d, block):
        return pltpu.make_async_remote_copy(
            src_ref=block, dst_ref=block, send_sem=y_send.at[e, d], recv_sem=y_recv.at[e, d],
            device_id=y_peer(e), device_id_type=MESH,
        )

    for d in range(1, n_z):
        z_copy(d, piece(z, y)).start()
    for e in range(1, n_y):
        y_copy(e, 0, piece(z, y)).start()

    adj_copy.wait()
    small = slots <= 8 and n_y * rows == tile

    def live(k):
        return jnp.where(k < count_ref[0, 0], coord_ref[0, 0, k], -1)

    if small:
        for s in range(n_src):
            for t in range(n_tgt):
                block = jnp.zeros((tile, tile), F32)
                for k in range(slots):
                    keep = jnp.where(live(k) == t * n_src + s, 1.0, 0.0).astype(F32)
                    block = block + adj[k].astype(F32) * keep
                dense[s, pl.ds(t * tile, tile), :] = block.astype(BF16)

    for d in range(n_z):
        z_from = back(z, d, n_z)
        if d > 0:
            z_copy(d, piece(z_from, y)).wait_recv()
            for e in range(1, n_y):
                y_copy(e, d, piece(z_from, y)).start()
    for d in range(n_z):
        z_from = back(z, d, n_z)
        for e in range(1, n_y):
            y_copy(e, d, piece(z_from, back(y, e, n_y))).wait_recv()
        if small:
            values = feats[pl.ds(pl.multiple_of(z_from * tile, tile), tile), :]
            product = jnp.dot(dense[z_from], values, preferred_element_type=F32)
            total[...] = product if d == 0 else total[...] + product

    if not small:
        total[...] = jnp.zeros_like(total)

        def add_slot(k, carry):
            at = live(k)
            source = jnp.where(at < 0, 0, lax.rem(at, n_src))
            values = feats[pl.ds(pl.multiple_of(source * tile, tile), tile), :]
            product = jnp.dot(adj[k], values, preferred_element_type=F32)
            for t in range(n_tgt):
                own = jnp.logical_and(at >= t * n_src, at < (t + 1) * n_src)
                total[pl.ds(t * tile, tile), :] += product * jnp.where(own, 1.0, 0.0).astype(F32)
            return carry

        lax.fori_loop(0, slots, add_slot, 0)

    def row_copy(d):
        return pltpu.make_async_remote_copy(
            src_ref=stage.at[d - 1], dst_ref=parts.at[d - 1],
            send_sem=row_send.at[d - 1], recv_sem=row_recv.at[d - 1],
            device_id=row_peer(d), device_id_type=MESH,
        )

    def block_of(r):
        return total[pl.ds(pl.multiple_of(r * rows, rows), rows), :]

    for d in range(1, n_row):
        stage[d - 1] = block_of(lax.rem(row + d, n_row)).astype(stage.dtype)
        row_copy(d).start()
    weight_copy.wait()
    hidden = block_of(row)
    for d in range(1, n_row):
        row_copy(d).wait_recv()
        hidden = hidden + parts[d - 1].astype(F32)
    mixed = jnp.dot(hidden.astype(BF16), weight[...], preferred_element_type=F32)
    out_ref[...] = jnp.maximum(mixed, 0.0).astype(out_ref.dtype)

    for d in range(1, n_z):
        z_copy(d, piece(z, y)).wait_send()
    for d in range(n_z):
        for e in range(1, n_y):
            y_copy(e, d, piece(back(z, d, n_z), y)).wait_send()
    for d in range(1, n_row):
        row_copy(d).wait_send()


def solution(mesh):
    n_row, n_col = mesh.shape["row"], mesh.shape["col"]
    n_y = max(1, n_row // 2)
    if n_col % n_y:
        n_y = 1
    n_z = n_col // n_y

    def on_device(features, adj_tiles, tile_coord, tile_count, weight):
        rows, width = features.shape
        slots, tile = adj_tiles.shape[2:4]
        n_tgt = n_row * rows // tile
        n_src = n_col * rows // tile
        small = slots <= 8 and n_y * rows == tile
        any_space = pl.BlockSpec(memory_space=pl.ANY)
        scalars = pl.BlockSpec(memory_space=pltpu.SMEM)
        dma = pltpu.SemaphoreType.DMA
        return pl.pallas_call(
            functools.partial(kernel, n_row, n_z, n_y),
            out_shape=jax.ShapeDtypeStruct((rows, weight.shape[1]), BF16),
            in_specs=[any_space, any_space, scalars, scalars, any_space],
            out_specs=pl.BlockSpec(memory_space=pltpu.VMEM),
            scratch_shapes=[
                pltpu.VMEM((n_col * rows, width), BF16),
                pltpu.VMEM((slots, tile, tile), BF16),
                pltpu.VMEM(weight.shape, BF16),
                pltpu.VMEM((n_src, n_tgt * tile, tile) if small else (1, 16, 128), BF16),
                pltpu.VMEM((n_tgt * tile, width), F32),
                pltpu.VMEM((n_row - 1, rows, width), BF16),
                pltpu.VMEM((n_row - 1, rows, width), BF16),
                dma, dma, dma,
                dma((n_z,)), dma((n_z,)),
                dma((max(n_y, 1), n_z)), dma((max(n_y, 1), n_z)),
                dma((n_row - 1,)), dma((n_row - 1,)),
            ],
            compiler_params=pltpu.CompilerParams(
                collective_id=0, has_side_effects=True, vmem_limit_bytes=32 * 2**20
            ),
        )(features, adj_tiles, tile_coord, tile_count, weight)

    return jax.shard_map(
        on_device,
        mesh=mesh,
        in_specs=(
            P(("row", "col"), None),
            P("row", "col", None, None, None),
            P("row", "col", None),
            P("row", "col"),
            P(),
        ),
        out_specs=P(("col", "row"), None),
        check_vma=False,
    )
```

time: 90.4 us -> 21.3 us (0.24)
  blocking collectives: 32.9 us -> 0 us
  waiting for transfers between devices: 21.2 us -> 0 us
  Pallas kernels: 0 us -> 17.2 us
  between operations: 14.1 us -> 0.69 us
  loops' own time: 11.8 us -> 0 us
  matrix products: 3.75 us -> 0 us
  other arithmetic: 2.9 us -> 0 us
    all_gather x1 -> x0, blocking collectives: 32.9 us -> none  [on_device(): gathered = lax.all_gather(features, 'col', axis=0, tiled=True)]
    reduce_scatter x1 -> x0, waiting for transfers between devices: 21.2 us -> none  [on_device(): lax.psum_scatter(partial_value, 'row', scatter_dimension=0, tiled=True)]
    pallas_call x0 -> x1, Pallas kernels: none -> 17.2 us  [on_device(): pl.pallas_call(functools.partial(kernel, n_row, n_z, n_y), out_shape=jax....]
    another operation x1 -> x0, loops' own time: 11.8 us -> none  [on_device(): total, unused = lax.scan(add_group, start_total, inputs)]
    dot_general x4 -> x0, matrix products: 3.75 us -> none  [the longest x3 2.14 us: add_group(): jnp.einsum('kij,kjf->kif', tile_group, feat_rows, preferred_element_type=...]
    another operation x3 -> x0, other arithmetic: 2.11 us -> none
    dynamic_slice x3 -> x0, local copies, waits for them, and re-layouts: 2 us -> none  [on_device(): total, unused = lax.scan(add_group, start_total, inputs)]
    unnamed x8 -> x9, local copies, waits for them, and re-layouts: 1.31 us -> 3.17 us
  transfers between devices with their start and end apart: 1 -> 0, of which waited for: 1 -> 0; matrix products, arithmetic and copies ran while one was open for 0% -> 0% of each run, Pallas kernels for 0% -> 0%
where the time goes in v1:
time: 21.3 us; the launch traced here: 21.1 us
  Pallas kernels  17.2 us (81%)
  local copies, waits for them, and re-layouts  3.17 us (15%)
  between operations  0.69 us (3%)
    pallas_call x1, Pallas kernels, on_device(): pl.pallas_call(functools.partial(kernel, n_row, n_z, n_y), out_shape=jax....  17.2 us
    unnamed x9, local copies, waits for them, and re-layouts  3.17 us

profile of v1, /device:TPU:0, one launch (start us, length us, event | category | flops | bytes accessed | tf_op | source)
XLA Modules:
  0.0 21.1 jit_solution(977998692294090074)
XLA Ops:
  0.0 0.0 copy-start.3
  0.7 0.0 copy-done.3
  0.7 0.0 copy-start
  0.7 0.9 %copy-done = bf16[256,256]{1,0:T(8,128)(2,1)S(1)} copy-done((bf16[256,256]{1,0:T(8,128)(2,1)S(1)}, bf16[256,256]{1,0:T(8,128)(2,1)}, u32[]{:S(2)}) %copy-start) | copy-done | bytes 131096
  1.6 0.0 copy-start.1
  1.6 0.9 %copy-done.1 = bf16[1,1,3,128,128]{4,3,2,1,0:T(8,128)(2,1)S(1)} copy-done((bf16[1,1,3,128,128]{4,3,2,1,0:T(8,128)(2,1)S(1)}, bf16[1,1,3,128,128]{4,3,2,1,0:T(8,128)(2,1)}, u32[]{:S(2)}) %copy-start.1) | copy-done | bytes 98328
  2.5 0.0 copy-start.2
  2.5 0.8 %copy-done.2 = bf16[64,256]{1,0:T(8,128)(2,1)S(1)} copy-done((bf16[64,256]{1,0:T(8,128)(2,1)S(1)}, bf16[64,256]{1,0:T(8,128)(2,1)}, u32[]{:S(2)}) %copy-start.2) | copy-done | bytes 32792
  3.2 17.2 %shard_map.55 = bf16[64,256]{1,0:T(8,128)(2,1)S(1)} custom-call(bf16[64,256]{1,0:T(8,128)(2,1)S(1)} %copy-done.2, bf16[1,1,3,128,128]{4,3,2,1,0:T(8,128)(2,1)S(1)} %copy-done.1, s32[1,1,3]{2,1,0:T(1,128)S(1)} %copy-done.3, s32[1,1]{1,0:T(1,128)S(6)} %copy.7.count_ref, bf16[256,256]{1,0:T(8,128)(2,1)S(1)} %copy-done), custom_call_target="tpu_custom_call" | custom-call | tf_op jit(solution)/shard_map/pallas_call | solution.py:167
  20.5 0.6 %copy.8 = bf16[64,256]{1,0:T(8,128)(2,1)} copy(bf16[64,256]{1,0:T(8,128)(2,1)S(1)} %shard_map.55) | data formatting | bytes 65536
Async XLA Ops:
  0.0 0.7 %copy-start.3 = (s32[1,1,3]{2,1,0:T(1,128)S(1)}, s32[1,1,3]{2,1,0:T(1,128)}, u32[]{:S(2)}) copy-start(s32[1,1,3]{2,1,0:T(1,128)} %coord_ref.1) | copy-start | bytes 40
  0.7 0.9 %copy-start = (bf16[256,256]{1,0:T(8,128)(2,1)S(1)}, bf16[256,256]{1,0:T(8,128)(2,1)}, u32[]{:S(2)}) copy-start(bf16[256,256]{1,0:T(8,128)(2,1)} %w_ref.1) | copy-start | bytes 393220
  1.6 0.9 %copy-start.1 = (bf16[1,1,3,128,128]{4,3,2,1,0:T(8,128)(2,1)S(1)}, bf16[1,1,3,128,128]{4,3,2,1,0:T(8,128)(2,1)}, u32[]{:S(2)}) copy-start(bf16[1,1,3,128,128]{4,3,2,1,0:T(8,128)(2,1)} %adj_ref.1) | copy-start | bytes 294916
  2.5 0.8 %copy-start.2 = (bf16[64,256]{1,0:T(8,128)(2,1)S(1)}, bf16[64,256]{1,0:T(8,128)(2,1)}, u32[]{:S(2)}) copy-start(bf16[64,256]{1,0:T(8,128)(2,1)} %x_ref.1) | copy-start | bytes 98308

commit v2 on v1

--- a/solution.py
+++ b/solution.py
@@ -15,8 +15,8 @@
 def kernel(
     n_row, n_z, n_y,
     x_ref, adj_ref, coord_ref, count_ref, w_ref, out_ref,
-    feats, adj, weight, dense, total, stage, parts,
-    own_sem, adj_sem, weight_sem, z_send, z_recv, y_send, y_recv, row_send, row_recv,
+    feats, adj, weight, coord, count, dense, total, stage, parts,
+    int_sems, own_sem, adj_sem, weight_sem, z_send, z_recv, y_send, y_recv, row_send, row_recv,
 ):
     row, col = lax.axis_index("row"), lax.axis_index("col")
     z, y = col // n_y, col % n_y
@@ -42,6 +42,10 @@
 
     own_copy = pltpu.make_async_copy(x_ref, piece(z, y), own_sem)
     own_copy.start()
+    coord_copy = pltpu.make_async_copy(coord_ref, coord, int_sems.at[0])
+    coord_copy.start()
+    count_copy = pltpu.make_async_copy(count_ref, count, int_sems.at[1])
+    count_copy.start()
     adj_copy = pltpu.make_async_copy(adj_ref.at[0, 0], adj, adj_sem)
     adj_copy.start()
     weight_copy = pltpu.make_async_copy(w_ref, weight, weight_sem)
@@ -73,11 +77,13 @@
     for e in range(1, n_y):
         y_copy(e, 0, piece(z, y)).start()
 
+    coord_copy.wait()
+    count_copy.wait()
     adj_copy.wait()
     small = slots <= 8 and n_y * rows == tile
 
     def live(k):
-        return jnp.where(k < count_ref[0, 0], coord_ref[0, 0, k], -1)
+        return jnp.where(k < count[0, 0], coord[0, 0, k], -1)
 
     if small:
         for s in range(n_src):
@@ -161,29 +167,30 @@
         n_tgt = n_row * rows // tile
         n_src = n_col * rows // tile
         small = slots <= 8 and n_y * rows == tile
-        any_space = pl.BlockSpec(memory_space=pl.ANY)
-        scalars = pl.BlockSpec(memory_space=pltpu.SMEM)
+        in_hbm = pl.BlockSpec(memory_space=pltpu.HBM)
         dma = pltpu.SemaphoreType.DMA
         return pl.pallas_call(
             functools.partial(kernel, n_row, n_z, n_y),
             out_shape=jax.ShapeDtypeStruct((rows, weight.shape[1]), BF16),
-            in_specs=[any_space, any_space, scalars, scalars, any_space],
+            in_specs=[in_hbm] * 5,
             out_specs=pl.BlockSpec(memory_space=pltpu.VMEM),
             scratch_shapes=[
                 pltpu.VMEM((n_col * rows, width), BF16),
                 pltpu.VMEM((slots, tile, tile), BF16),
                 pltpu.VMEM(weight.shape, BF16),
+                pltpu.SMEM(tile_coord.shape, jnp.int32),
+                pltpu.SMEM(tile_count.shape, jnp.int32),
                 pltpu.VMEM((n_src, n_tgt * tile, tile) if small else (1, 16, 128), BF16),
                 pltpu.VMEM((n_tgt * tile, width), F32),
                 pltpu.VMEM((n_row - 1, rows, width), BF16),
                 pltpu.VMEM((n_row - 1, rows, width), BF16),
-                dma, dma, dma,
+                dma((2,)), dma, dma, dma,
                 dma((n_z,)), dma((n_z,)),
                 dma((max(n_y, 1), n_z)), dma((max(n_y, 1), n_z)),
                 dma((n_row - 1,)), dma((n_row - 1,)),
             ],
             compiler_params=pltpu.CompilerParams(
-                collective_id=0, has_side_effects=True, vmem_limit_bytes=32 * 2**20
+                collective_id=0, has_side_effects=True, vmem_limit_bytes=64 * 2**20
             ),
         )(features, adj_tiles, tile_coord, tile_count, weight)
 

time: 21.3 us -> 19.2 us (0.901)
  local copies, waits for them, and re-layouts: 3.17 us -> 1.38 us
    unnamed x9 -> x1, local copies, waits for them, and re-layouts: 3.17 us -> 1.38 us
    pallas_call x1, Pallas kernels: 17.2 us -> 17 us  [on_device(): pl.pallas_call(functools.partial(kernel, n_row, n_z, n_y), out_shape=jax....]
where the time goes in v2:
time: 19.2 us; the launch traced here: 19 us
  Pallas kernels  17 us (89%)
  local copies, waits for them, and re-layouts  1.38 us (7%)
  between operations  0.66 us (3%)
    pallas_call x1, Pallas kernels, on_device(): pl.pallas_call(functools.partial(kernel, n_row, n_z, n_y), out_shape=jax....  17 us
    unnamed x1, local copies, waits for them, and re-layouts  1.38 us

profile of v2, /device:TPU:0, one launch (start us, length us, event | category | flops | bytes accessed | tf_op | source)
XLA Modules:
  0.0 19.0 jit_solution(3695423301275130674)
XLA Ops:
  0.7 17.0 %shard_map.55 = bf16[64,256]{1,0:T(8,128)(2,1)} custom-call(bf16[64,256]{1,0:T(8,128)(2,1)} %x_ref.1, bf16[1,1,3,128,128]{4,3,2,1,0:T(8,128)(2,1)} %adj_ref.1, s32[1,1,3]{2,1,0:T(1,128)} %coord_ref.1, s32[1,1]{1,0:T(1,128)S(6)} %copy.7.count_ref, bf16[256,256]{1,0:T(8,128)(2,1)} %w_ref.1), custom_call_target="tpu_custom_call" | custom-call | tf_op jit(solution)/shard_map/pallas_call | solution.py:172
  17.7 1.4 %copy.8 = bf16[64,256]{1,0:T(8,128)(2,1)} copy(bf16[64,256]{1,0:T(8,128)(2,1)} %shard_map.55) | data formatting | bytes 65536

commit v3 on v2

v3 whole, which is shorter than its diff:
```python
import functools

import jax
import jax.numpy as jnp
from jax import lax
from jax.experimental import pallas as pl
from jax.experimental.pallas import tpu as pltpu
from jax.sharding import PartitionSpec as P

MESH = pl.DeviceIdType.MESH
F32 = jnp.float32
BF16 = jnp.bfloat16


def kernel(
    n_row, n_z, n_y,
    x_ref, adj_ref, coord_ref, count_ref, w_ref, out_ref,
    feats, adj, weight, coord, count, dense, total, stage, parts,
    int_sems, own_sems, adj_sem, weight_sem, z_send, z_recv, y_send, y_recv, row_send, row_recv,
):
    row, col = lax.axis_index("row"), lax.axis_index("col")
    z, y = col // n_y, col % n_y
    slots, tile = adj_ref.shape[2], adj_ref.shape[3]
    rows = x_ref.shape[0]
    halves, _, width = feats.shape
    n_tgt = n_row * rows // tile
    n_src = n_z * n_y * rows // tile
    row_order = sorted(range(1, n_row), key=lambda d: d % 2)

    def piece(h, z_at, y_at):
        return feats.at[h, pl.ds(pl.multiple_of((z_at * n_y + y_at) * rows, rows), rows)]

    def z_peer(d):
        return {"col": lax.rem(z + d, n_z) * n_y + y}

    def y_peer(e):
        return {"col": z * n_y + lax.rem(y + e, n_y)}

    def row_peer(d):
        return {"row": lax.rem(row + d, n_row)}

    def back(at, d, n):
        return lax.rem(at + n - d, n)

    own_copies = [
        pltpu.make_async_copy(x_ref.at[:, pl.ds(h * width, width)], piece(h, z, y), own_sems.at[h])
        for h in range(halves)
    ]
    for copy in own_copies:
        copy.start()
    coord_copy = pltpu.make_async_copy(coord_ref, coord, int_sems.at[0])
    coord_copy.start()
    count_copy = pltpu.make_async_copy(count_ref, count, int_sems.at[1])
    count_copy.start()
    adj_copy = pltpu.make_async_copy(adj_ref.at[0, 0], adj, adj_sem)
    adj_copy.start()
    weight_copy = pltpu.make_async_copy(w_ref, weight, weight_sem)
    weight_copy.start()

    barrier = pltpu.get_barrier_semaphore()
    peers = [z_peer(d) for d in range(1, n_z)]
    peers += [y_peer(e) for e in range(1, n_y)]
    peers += [row_peer(d) for d in range(1, n_row)]
    for peer in peers:
        pl.semaphore_signal(barrier, inc=1, device_id=peer, device_id_type=MESH)
    pl.semaphore_wait(barrier, len(peers))

    def z_copy(h, d, block):
        return pltpu.make_async_remote_copy(
            src_ref=block, dst_ref=block, send_sem=z_send.at[h, d], recv_sem=z_recv.at[h, d],
            device_id=z_peer(d), device_id_type=MESH,
        )

    def y_copy(h, e, d, block):
        return pltpu.make_async_remote_copy(
            src_ref=block, dst_ref=block, send_sem=y_send.at[h, e, d], recv_sem=y_recv.at[h, e, d],
            device_id=y_peer(e), device_id_type=MESH,
        )

    for h in range(halves):
        own_copies[h].wait()
        for d in range(1, n_z):
            z_copy(h, d, piece(h, z, y)).start()
        for e in range(1, n_y):
            y_copy(h, e, 0, piece(h, z, y)).start()

    coord_copy.wait()
    count_copy.wait()
    adj_copy.wait()
    small = slots <= 8 and n_y * rows == tile

    def live(k):
        return jnp.where(k < count[0, 0], coord[0, 0, k], -1)

    if small:
        for s in range(n_src):
            for t in range(n_tgt):
                block = jnp.zeros((tile, tile), F32)
                for k in range(slots):
                    keep = jnp.where(live(k) == t * n_src + s, 1.0, 0.0).astype(F32)
                    block = block + adj[k].astype(F32) * keep
                dense[s, pl.ds(t * tile, tile), :] = block.astype(BF16)

    for h in range(halves):
        for d in range(1, n_z):
            block = piece(h, back(z, d, n_z), y)
            z_copy(h, d, block).wait_recv()
            for e in range(1, n_y):
                y_copy(h, e, d, block).start()

    def row_copy(h, d):
        return pltpu.make_async_remote_copy(
            src_ref=stage.at[h, d - 1], dst_ref=parts.at[h, d - 1],
            send_sem=row_send.at[h, d - 1], recv_sem=row_recv.at[h, d - 1],
            device_id=row_peer(d), device_id_type=MESH,
        )

    def block_of(h, r):
        return total[h, pl.ds(pl.multiple_of(r * rows, rows), rows), :]

    for h in range(halves):
        product = None
        for d in range(n_z):
            z_from = back(z, d, n_z)
            for e in range(1, n_y):
                y_copy(h, e, d, piece(h, z_from, back(y, e, n_y))).wait_recv()
            if small:
                values = feats[h, pl.ds(pl.multiple_of(z_from * tile, tile), tile), :]
                term = jnp.dot(dense[z_from], values, preferred_element_type=F32)
                product = term if d == 0 else product + term
        if small:
            total[h] = product
        else:
            total[h] = jnp.zeros(total.shape[1:], F32)

            def add_slot(k, carry):
                at = live(k)
                source = jnp.where(at < 0, 0, lax.rem(at, n_src))
                values = feats[h, pl.ds(pl.multiple_of(source * tile, tile), tile), :]
                term = jnp.dot(adj[k], values, preferred_element_type=F32)
                for t in range(n_tgt):
                    own = jnp.logical_and(at >= t * n_src, at < (t + 1) * n_src)
                    total[h, pl.ds(t * tile, tile), :] += term * jnp.where(own, 1.0, 0.0).astype(F32)
                return carry

            lax.fori_loop(0, slots, add_slot, 0)
        for d in row_order:
            stage[h, d - 1] = block_of(h, lax.rem(row + d, n_row)).astype(stage.dtype)
            row_copy(h, d).start()

    weight_copy.wait()
    mixed = None
    for h in range(halves):
        hidden = block_of(h, row)
        for d in reversed(row_order):
            row_copy(h, d).wait_recv()
            hidden = hidden + parts[h, d - 1].astype(F32)
        term = jnp.dot(
            hidden.astype(BF16), weight[pl.ds(h * width, width), :], preferred_element_type=F32
        )
        mixed = term if h == 0 else mixed + term
    out_ref[...] = jnp.maximum(mixed, 0.0).astype(out_ref.dtype)

    for h in range(halves):
        for d in range(1, n_z):
            z_copy(h, d, piece(h, z, y)).wait_send()
        for d in range(n_z):
            for e in range(1, n_y):
                y_copy(h, e, d, piece(h, back(z, d, n_z), y)).wait_send()
        for d in range(1, n_row):
            row_copy(h, d).wait_send()


def solution(mesh):
    n_row, n_col = mesh.shape["row"], mesh.shape["col"]
    n_y = max(1, n_row // 2)
    if n_col % n_y:
        n_y = 1
    n_z = n_col // n_y

    def on_device(features, adj_tiles, tile_coord, tile_count, weight):
        rows, width = features.shape
        slots, tile = adj_tiles.shape[2:4]
        n_tgt = n_row * rows // tile
        n_src = n_col * rows // tile
        small = slots <= 8 and n_y * rows == tile
        in_hbm = pl.BlockSpec(memory_space=pltpu.HBM)
        dma = pltpu.SemaphoreType.DMA
        halves = 2
        half = width // halves
        return pl.pallas_call(
            functools.partial(kernel, n_row, n_z, n_y),
            out_shape=jax.ShapeDtypeStruct((rows, weight.shape[1]), BF16),
            in_specs=[in_hbm] * 5,
            out_specs=pl.BlockSpec(memory_space=pltpu.VMEM),
            scratch_shapes=[
                pltpu.VMEM((halves, n_col * rows, half), BF16),
                pltpu.VMEM((slots, tile, tile), BF16),
                pltpu.VMEM(weight.shape, BF16),
                pltpu.SMEM(tile_coord.shape, jnp.int32),
                pltpu.SMEM(tile_count.shape, jnp.int32),
                pltpu.VMEM((n_src, n_tgt * tile, tile) if small else (1, 16, 128), BF16),
                pltpu.VMEM((halves, n_tgt * tile, half), F32),
                pltpu.VMEM((halves, n_row - 1, rows, half), BF16),
                pltpu.VMEM((halves, n_row - 1, rows, half), BF16),
                dma((2,)), dma((halves,)), dma, dma,
                dma((halves, n_z)), dma((halves, n_z)),
                dma((halves, n_y, n_z)), dma((halves, n_y, n_z)),
                dma((halves, n_row - 1)), dma((halves, n_row - 1)),
            ],
            compiler_params=pltpu.CompilerParams(
                collective_id=0, has_side_effects=True, vmem_limit_bytes=64 * 2**20
            ),
        )(features, adj_tiles, tile_coord, tile_count, weight)

    return jax.shard_map(
        on_device,
        mesh=mesh,
        in_specs=(
            P(("row", "col"), None),
            P("row", "col", None, None, None),
            P("row", "col", None),
            P("row", "col"),
            P(),
        ),
        out_specs=P(("col", "row"), None),
        check_vma=False,
    )
```

time: 19.2 us -> 19.2 us (level)
  no operation moved by 1% of the time
where the time goes in v3:
time: 19.2 us; the launch traced here: 19 us
  Pallas kernels  17 us (89%)
  local copies, waits for them, and re-layouts  1.38 us (7%)
  between operations  0.66 us (3%)
    pallas_call x1, Pallas kernels, on_device(): pl.pallas_call(functools.partial(kernel, n_row, n_z, n_y), out_shape=jax....  17 us
    unnamed x1, local copies, waits for them, and re-layouts  1.38 us

profile of v3, /device:TPU:0, one launch (start us, length us, event | category | flops | bytes accessed | tf_op | source)
XLA Modules:
  0.0 19.0 jit_solution(14969037002815810574)
XLA Ops:
  0.7 17.0 %shard_map.55 = bf16[64,256]{1,0:T(8,128)(2,1)} custom-call(bf16[64,256]{1,0:T(8,128)(2,1)} %x_ref.1, bf16[1,1,3,128,128]{4,3,2,1,0:T(8,128)(2,1)} %adj_ref.1, s32[1,1,3]{2,1,0:T(1,128)} %coord_ref.1, s32[1,1]{1,0:T(1,128)S(6)} %copy.7.count_ref, bf16[256,256]{1,0:T(8,128)(2,1)} %w_ref.1), custom_call_target="tpu_custom_call" | custom-call | tf_op jit(solution)/shard_map/pallas_call | solution.py:191
  17.6 1.4 %copy.8 = bf16[64,256]{1,0:T(8,128)(2,1)} copy(bf16[64,256]{1,0:T(8,128)(2,1)} %shard_map.55) | data formatting | bytes 65536

commit v4 on v3

--- a/solution.py
+++ b/solution.py
@@ -171,6 +171,178 @@
             row_copy(h, d).wait_send()
 
 
+def pair_kernel(
+    n_row, n_col,
+    x_ref, adj_ref, coord_ref, count_ref, w_ref, out_ref,
+    own, feats, adj, weight, coord, count, code, dense, total, stage, parts,
+    int_sems, own_sems, adj_sem, weight_sem,
+    pair_send, pair_recv, col_send, col_recv, row_send, row_recv,
+):
+    row, col = lax.axis_index("row"), lax.axis_index("col")
+    side = col % 2
+    pair = col + 1 - 2 * side
+    slots, tile = adj_ref.shape[2], adj_ref.shape[3]
+    rows, half = x_ref.shape[0], feats.shape[1]
+    n_tgt, n_src = n_row * rows // tile, n_col * rows // tile
+    targets = n_tgt * tile
+
+    def piece(c):
+        return feats.at[pl.ds(pl.multiple_of(c * rows, rows), rows)]
+
+    def columns(h):
+        return x_ref.at[:, pl.ds(pl.multiple_of(h * half, half), half)]
+
+    coord_copy = pltpu.make_async_copy(coord_ref, coord, int_sems.at[0])
+    count_copy = pltpu.make_async_copy(count_ref, count, int_sems.at[1])
+    adj_copy = pltpu.make_async_copy(adj_ref.at[0, 0], adj.at[0], adj_sem)
+    weight_copy = pltpu.make_async_copy(w_ref, weight, weight_sem)
+    own_copies = [pltpu.make_async_copy(columns(h), own.at[h], own_sems.at[h]) for h in range(2)]
+    own_copies.append(pltpu.make_async_copy(columns(side), piece(col), own_sems.at[2]))
+    for copy in own_copies + [coord_copy, count_copy, adj_copy, weight_copy]:
+        copy.start()
+
+    row_peers = [(e, d) for d in range(n_row) for e in range(2) if e + d > 0]
+    row_peers.sort(key=lambda ed: (ed[1] % 2, -ed[1]))
+
+    def row_peer(e, d):
+        return {"row": lax.rem(row + d, n_row), "col": pair if e else col}
+
+    barrier = pltpu.get_barrier_semaphore()
+    peers = [{"col": lax.rem(col + d, n_col)} for d in range(1, n_col)]
+    peers += [row_peer(e, d) for e, d in row_peers if d > 0]
+    for peer in peers:
+        pl.semaphore_signal(barrier, inc=1, device_id=peer, device_id_type=MESH)
+    pl.semaphore_wait(barrier, len(peers))
+
+    pair_adj = pltpu.make_async_remote_copy(
+        src_ref=adj_ref.at[0, 0], dst_ref=adj.at[1], send_sem=pair_send.at[0],
+        recv_sem=pair_recv.at[0], device_id={"col": pair}, device_id_type=MESH,
+    )
+    pair_adj.start()
+    for copy in own_copies:
+        copy.wait()
+
+    def col_copy(d):
+        return pltpu.make_async_remote_copy(
+            src_ref=own.at[lax.rem(side + d, 2)], dst_ref=piece(col), send_sem=col_send.at[d],
+            recv_sem=col_recv.at[col], device_id={"col": lax.rem(col + d, n_col)},
+            device_id_type=MESH,
+        )
+
+    for d in range(1, n_col):
+        col_copy(d).start()
+
+    coord_copy.wait()
+    count_copy.wait()
+    for k in range(slots):
+        at = jnp.where(k < count[0, 0], coord[0, 0, k], -1)
+        code[0, pl.ds(k, 1), :] = jnp.full((1, tile), at, jnp.int32)
+    pair_code = pltpu.make_async_remote_copy(
+        src_ref=code.at[0], dst_ref=code.at[1], send_sem=pair_send.at[1],
+        recv_sem=pair_recv.at[1], device_id={"col": pair}, device_id_type=MESH,
+    )
+    pair_code.start()
+
+    def spread(e):
+        for s in range(n_src):
+            for t in range(n_tgt):
+                block = jnp.zeros((tile, tile), F32)
+                for k in range(slots):
+                    keep = jnp.where(code[e, pl.ds(k, 1), :] == t * n_src + s, 1.0, 0.0).astype(F32)
+                    block = block + adj[e, k].astype(F32) * keep
+                dense[s, pl.ds(e * targets + t * tile, tile), :] = block.astype(BF16)
+
+    adj_copy.wait()
+    spread(0)
+    pair_adj.wait_recv()
+    pair_code.wait_recv()
+    spread(1)
+
+    def arrived(c):
+        pltpu.make_async_remote_copy(
+            src_ref=own.at[0], dst_ref=piece(c), send_sem=col_send.at[0],
+            recv_sem=col_recv.at[c], device_id={"col": pair}, device_id_type=MESH,
+        ).wait_recv()
+
+    product = None
+    for q in range(n_src):
+        s = lax.rem(col // 2 + q, n_src)
+        if q == 0:
+            arrived(pair)
+        else:
+            arrived(2 * s)
+            arrived(2 * s + 1)
+        values = feats[pl.ds(pl.multiple_of(s * tile, tile), tile), :]
+        term = jnp.dot(dense[s], values, preferred_element_type=F32)
+        product = term if q == 0 else product + term
+    total[...] = product
+
+    def row_copy(e, d):
+        return pltpu.make_async_remote_copy(
+            src_ref=stage.at[e, d], dst_ref=parts.at[e, d], send_sem=row_send.at[e, d],
+            recv_sem=row_recv.at[e, d], device_id=row_peer(e, d), device_id_type=MESH,
+        )
+
+    def block_of(e, r):
+        return total[pl.ds(pl.multiple_of(e * targets + r * rows, rows), rows), :]
+
+    for e, d in row_peers:
+        stage[e, d] = block_of(e, lax.rem(row + d, n_row)).astype(stage.dtype)
+        row_copy(e, d).start()
+    weight_copy.wait()
+    hidden = [block_of(0, row), jnp.zeros((rows, half), F32)]
+    for e, d in reversed(row_peers):
+        row_copy(e, d).wait_recv()
+        hidden[e] = hidden[e] + parts[e, d].astype(F32)
+
+    def weight_rows(h):
+        return weight[pl.ds(pl.multiple_of(h * half, half), half), :]
+
+    mixed = jnp.dot(hidden[0].astype(BF16), weight_rows(side), preferred_element_type=F32)
+    mixed += jnp.dot(hidden[1].astype(BF16), weight_rows(1 - side), preferred_element_type=F32)
+    out_ref[...] = jnp.maximum(mixed, 0.0).astype(out_ref.dtype)
+
+    pair_adj.wait_send()
+    pair_code.wait_send()
+    for d in range(1, n_col):
+        col_copy(d).wait_send()
+    for e, d in row_peers:
+        row_copy(e, d).wait_send()
+
+
+def pair_call(n_row, n_col, features, adj_tiles, tile_coord, tile_count, weight):
+    rows, width = features.shape
+    slots, tile = adj_tiles.shape[2:4]
+    targets, n_src, half = n_row * rows, n_col * rows // tile, width // 2
+    dma = pltpu.SemaphoreType.DMA
+    return pl.pallas_call(
+        functools.partial(pair_kernel, n_row, n_col),
+        out_shape=jax.ShapeDtypeStruct((rows, weight.shape[1]), BF16),
+        in_specs=[pl.BlockSpec(memory_space=pltpu.HBM)] * 5,
+        out_specs=pl.BlockSpec(memory_space=pltpu.VMEM),
+        scratch_shapes=[
+            pltpu.VMEM((2, rows, half), BF16),
+            pltpu.VMEM((n_col * rows, half), BF16),
+            pltpu.VMEM((2, slots, tile, tile), BF16),
+            pltpu.VMEM(weight.shape, BF16),
+            pltpu.SMEM(tile_coord.shape, jnp.int32),
+            pltpu.SMEM(tile_count.shape, jnp.int32),
+            pltpu.VMEM((2, 8, tile), jnp.int32),
+            pltpu.VMEM((n_src, 2 * targets, tile), BF16),
+            pltpu.VMEM((2 * targets, half), F32),
+            pltpu.VMEM((2, n_row, rows, half), BF16),
+            pltpu.VMEM((2, n_row, rows, half), BF16),
+            dma((2,)), dma((3,)), dma, dma,
+            dma((2,)), dma((2,)),
+            dma((n_col,)), dma((n_col,)),
+            dma((2, n_row)), dma((2, n_row)),
+        ],
+        compiler_params=pltpu.CompilerParams(
+            collective_id=0, has_side_effects=True, vmem_limit_bytes=64 * 2**20
+        ),
+    )(features, adj_tiles, tile_coord, tile_count, weight)
+
+
 def solution(mesh):
     n_row, n_col = mesh.shape["row"], mesh.shape["col"]
     n_y = max(1, n_row // 2)
@@ -183,6 +355,9 @@
         slots, tile = adj_tiles.shape[2:4]
         n_tgt = n_row * rows // tile
         n_src = n_col * rows // tile
+        paired = slots <= 8 and 2 * rows == tile and width == 2 * tile and n_col % 2 == 0
+        if paired:
+            return pair_call(n_row, n_col, features, adj_tiles, tile_coord, tile_count, weight)
         small = slots <= 8 and n_y * rows == tile
         in_hbm = pl.BlockSpec(memory_space=pltpu.HBM)
         dma = pltpu.SemaphoreType.DMA

time: 19.2 us -> 19.2 us (level)
  no operation moved by 1% of the time
where the time goes in v4:
time: 19.2 us; the launch traced here: 19 us
  Pallas kernels  17 us (89%)
  local copies, waits for them, and re-layouts  1.38 us (7%)
  between operations  0.66 us (3%)
    pallas_call x1, Pallas kernels, pair_call(): pl.pallas_call(functools.partial(pair_kernel, n_row, n_col), out_shape=ja...  17 us
    unnamed x1, local copies, waits for them, and re-layouts  1.38 us

profile of v4, /device:TPU:0, one launch (start us, length us, event | category | flops | bytes accessed | tf_op | source)
XLA Modules:
  0.0 19.0 jit_solution(5214116215351133162)
XLA Ops:
  0.7 17.0 %shard_map.55 = bf16[64,256]{1,0:T(8,128)(2,1)} custom-call(bf16[64,256]{1,0:T(8,128)(2,1)} %x_ref.1, bf16[1,1,3,128,128]{4,3,2,1,0:T(8,128)(2,1)} %adj_ref.1, s32[1,1,3]{2,1,0:T(1,128)} %coord_ref.1, s32[1,1]{1,0:T(1,128)S(6)} %copy.7.count_ref, bf16[256,256]{1,0:T(8,128)(2,1)} %w_ref.1), custom_call_target="tpu_custom_call" | custom-call | tf_op jit(solution)/shard_map/pallas_call | solution.py:318
  17.6 1.4 %copy.8 = bf16[64,256]{1,0:T(8,128)(2,1)} copy(bf16[64,256]{1,0:T(8,128)(2,1)} %shard_map.55) | data formatting | bytes 65536

commit v5 on v4

--- a/solution.py
+++ b/solution.py
@@ -174,8 +174,8 @@
 def pair_kernel(
     n_row, n_col,
     x_ref, adj_ref, coord_ref, count_ref, w_ref, out_ref,
-    own, feats, adj, weight, coord, count, code, dense, total, stage, parts,
-    int_sems, own_sems, adj_sem, weight_sem,
+    own, feats, adj, weight, coord, code, dense, total, stage, parts,
+    coord_sem, own_sems, adj_sem, weight_sem,
     pair_send, pair_recv, col_send, col_recv, row_send, row_recv,
 ):
     row, col = lax.axis_index("row"), lax.axis_index("col")
@@ -192,15 +192,11 @@
     def columns(h):
         return x_ref.at[:, pl.ds(pl.multiple_of(h * half, half), half)]
 
-    coord_copy = pltpu.make_async_copy(coord_ref, coord, int_sems.at[0])
-    count_copy = pltpu.make_async_copy(count_ref, count, int_sems.at[1])
+    coord_copy = pltpu.make_async_copy(coord_ref, coord, coord_sem)
     adj_copy = pltpu.make_async_copy(adj_ref.at[0, 0], adj.at[0], adj_sem)
     weight_copy = pltpu.make_async_copy(w_ref, weight, weight_sem)
     own_copies = [pltpu.make_async_copy(columns(h), own.at[h], own_sems.at[h]) for h in range(2)]
     own_copies.append(pltpu.make_async_copy(columns(side), piece(col), own_sems.at[2]))
-    for copy in own_copies + [coord_copy, count_copy, adj_copy, weight_copy]:
-        copy.start()
-
     row_peers = [(e, d) for d in range(n_row) for e in range(2) if e + d > 0]
     row_peers.sort(key=lambda ed: (ed[1] % 2, -ed[1]))
 
@@ -212,6 +208,8 @@
     peers += [row_peer(e, d) for e, d in row_peers if d > 0]
     for peer in peers:
         pl.semaphore_signal(barrier, inc=1, device_id=peer, device_id_type=MESH)
+    for copy in own_copies + [coord_copy, adj_copy, weight_copy]:
+        copy.start()
     pl.semaphore_wait(barrier, len(peers))
 
     pair_adj = pltpu.make_async_remote_copy(
@@ -233,9 +231,8 @@
         col_copy(d).start()
 
     coord_copy.wait()
-    count_copy.wait()
     for k in range(slots):
-        at = jnp.where(k < count[0, 0], coord[0, 0, k], -1)
+        at = jnp.where(k < count_ref[0, 0], coord[0, 0, k], -1)
         code[0, pl.ds(k, 1), :] = jnp.full((1, tile), at, jnp.int32)
     pair_code = pltpu.make_async_remote_copy(
         src_ref=code.at[0], dst_ref=code.at[1], send_sem=pair_send.at[1],
@@ -310,15 +307,20 @@
         row_copy(e, d).wait_send()
 
 
+def hbm(array):
+    return pltpu.with_memory_space_constraint(array, pltpu.HBM)
+
+
 def pair_call(n_row, n_col, features, adj_tiles, tile_coord, tile_count, weight):
     rows, width = features.shape
     slots, tile = adj_tiles.shape[2:4]
     targets, n_src, half = n_row * rows, n_col * rows // tile, width // 2
     dma = pltpu.SemaphoreType.DMA
+    in_hbm = pl.BlockSpec(memory_space=pltpu.HBM)
     return pl.pallas_call(
         functools.partial(pair_kernel, n_row, n_col),
         out_shape=jax.ShapeDtypeStruct((rows, weight.shape[1]), BF16),
-        in_specs=[pl.BlockSpec(memory_space=pltpu.HBM)] * 5,
+        in_specs=[in_hbm, in_hbm, in_hbm, pl.BlockSpec(memory_space=pltpu.SMEM), in_hbm],
         out_specs=pl.BlockSpec(memory_space=pltpu.VMEM),
         scratch_shapes=[
             pltpu.VMEM((2, rows, half), BF16),
@@ -326,21 +328,20 @@
             pltpu.VMEM((2, slots, tile, tile), BF16),
             pltpu.VMEM(weight.shape, BF16),
             pltpu.SMEM(tile_coord.shape, jnp.int32),
-            pltpu.SMEM(tile_count.shape, jnp.int32),
             pltpu.VMEM((2, 8, tile), jnp.int32),
             pltpu.VMEM((n_src, 2 * targets, tile), BF16),
             pltpu.VMEM((2 * targets, half), F32),
             pltpu.VMEM((2, n_row, rows, half), BF16),
             pltpu.VMEM((2, n_row, rows, half), BF16),
-            dma((2,)), dma((3,)), dma, dma,
+            dma, dma((3,)), dma, dma,
             dma((2,)), dma((2,)),
             dma((n_col,)), dma((n_col,)),
             dma((2, n_row)), dma((2, n_row)),
         ],
         compiler_params=pltpu.CompilerParams(
-            collective_id=0, has_side_effects=True, vmem_limit_bytes=64 * 2**20
+            collective_id=0, has_side_effects=True, vmem_limit_bytes=32 * 2**20
         ),
-    )(features, adj_tiles, tile_coord, tile_count, weight)
+    )(hbm(features), hbm(adj_tiles), hbm(tile_coord), tile_count, hbm(weight))
 
 
 def solution(mesh):
@@ -384,9 +385,9 @@
                 dma((halves, n_row - 1)), dma((halves, n_row - 1)),
             ],
             compiler_params=pltpu.CompilerParams(
-                collective_id=0, has_side_effects=True, vmem_limit_bytes=64 * 2**20
+                collective_id=0, has_side_effects=True, vmem_limit_bytes=32 * 2**20
             ),
-        )(features, adj_tiles, tile_coord, tile_count, weight)
+        )(hbm(features), hbm(adj_tiles), hbm(tile_coord), tile_count, hbm(weight))
 
     return jax.shard_map(
         on_device,

time: 19.2 us -> 17.8 us (0.927)
  local copies, waits for them, and re-layouts: 1.38 us -> 0.62 us
  Pallas kernels: 17 us -> 16.4 us
    unnamed x1, local copies, waits for them, and re-layouts: 1.38 us -> 0.62 us
    pallas_call x1, Pallas kernels: 17 us -> 16.4 us  [pair_call(): pl.pallas_call(functools.partial(pair_kernel, n_row, n_col), out_shape=ja...]
where the time goes in v5:
time: 17.8 us; the launch traced here: 17.6 us
  Pallas kernels  16.4 us (92%)
  between operations  0.66 us (4%)
  local copies, waits for them, and re-layouts  0.62 us (3%)
    pallas_call x1, Pallas kernels, pair_call(): pl.pallas_call(functools.partial(pair_kernel, n_row, n_col), out_shape=ja...  16.4 us
    unnamed x1, local copies, waits for them, and re-layouts  0.62 us

profile of v5, /device:TPU:0, one launch (start us, length us, event | category | flops | bytes accessed | tf_op | source)
XLA Modules:
  0.0 17.6 jit_solution(6816680407435162692)
XLA Ops:
  0.7 16.4 %shard_map.55 = bf16[64,256]{1,0:T(8,128)(2,1)S(1)} custom-call(bf16[64,256]{1,0:T(8,128)(2,1)} %x_ref.1, bf16[1,1,3,128,128]{4,3,2,1,0:T(8,128)(2,1)} %adj_ref.1, s32[1,1,3]{2,1,0:T(1,128)} %coord_ref.1, s32[1,1]{1,0:T(1,128)S(6)} %copy.7.count_ref, bf16[256,256]{1,0:T(8,128)(2,1)} %w_ref.1), custom_call_target="tpu_custom_call" | custom-call | tf_op jit(solution)/shard_map/pallas_call | solution.py:320
  17.0 0.6 %copy.8 = bf16[64,256]{1,0:T(8,128)(2,1)} copy(bf16[64,256]{1,0:T(8,128)(2,1)S(1)} %shard_map.55) | data formatting | bytes 65536

commit v6 on v5

--- a/solution.py
+++ b/solution.py
@@ -174,8 +174,8 @@
 def pair_kernel(
     n_row, n_col,
     x_ref, adj_ref, coord_ref, count_ref, w_ref, out_ref,
-    own, feats, adj, weight, coord, code, dense, total, stage, parts,
-    coord_sem, own_sems, adj_sem, weight_sem,
+    feats, adj, weight, coord, code, dense, total, stage, parts,
+    coord_sem, own_sem, adj_sem, weight_sem,
     pair_send, pair_recv, col_send, col_recv, row_send, row_recv,
 ):
     row, col = lax.axis_index("row"), lax.axis_index("col")
@@ -195,8 +195,7 @@
     coord_copy = pltpu.make_async_copy(coord_ref, coord, coord_sem)
     adj_copy = pltpu.make_async_copy(adj_ref.at[0, 0], adj.at[0], adj_sem)
     weight_copy = pltpu.make_async_copy(w_ref, weight, weight_sem)
-    own_copies = [pltpu.make_async_copy(columns(h), own.at[h], own_sems.at[h]) for h in range(2)]
-    own_copies.append(pltpu.make_async_copy(columns(side), piece(col), own_sems.at[2]))
+    own_copy = pltpu.make_async_copy(columns(side), piece(col), own_sem)
     row_peers = [(e, d) for d in range(n_row) for e in range(2) if e + d > 0]
     row_peers.sort(key=lambda ed: (ed[1] % 2, -ed[1]))
 
@@ -208,7 +207,7 @@
     peers += [row_peer(e, d) for e, d in row_peers if d > 0]
     for peer in peers:
         pl.semaphore_signal(barrier, inc=1, device_id=peer, device_id_type=MESH)
-    for copy in own_copies + [coord_copy, adj_copy, weight_copy]:
+    for copy in (coord_copy, adj_copy, own_copy, weight_copy):
         copy.start()
     pl.semaphore_wait(barrier, len(peers))
 
@@ -216,19 +215,17 @@
         src_ref=adj_ref.at[0, 0], dst_ref=adj.at[1], send_sem=pair_send.at[0],
         recv_sem=pair_recv.at[0], device_id={"col": pair}, device_id_type=MESH,
     )
-    pair_adj.start()
-    for copy in own_copies:
-        copy.wait()
 
     def col_copy(d):
         return pltpu.make_async_remote_copy(
-            src_ref=own.at[lax.rem(side + d, 2)], dst_ref=piece(col), send_sem=col_send.at[d],
+            src_ref=columns(lax.rem(side + d, 2)), dst_ref=piece(col), send_sem=col_send.at[d],
             recv_sem=col_recv.at[col], device_id={"col": lax.rem(col + d, n_col)},
             device_id_type=MESH,
         )
 
     for d in range(1, n_col):
         col_copy(d).start()
+    pair_adj.start()
 
     coord_copy.wait()
     for k in range(slots):
@@ -257,10 +254,11 @@
 
     def arrived(c):
         pltpu.make_async_remote_copy(
-            src_ref=own.at[0], dst_ref=piece(c), send_sem=col_send.at[0],
+            src_ref=columns(0), dst_ref=piece(c), send_sem=col_send.at[0],
             recv_sem=col_recv.at[c], device_id={"col": pair}, device_id_type=MESH,
         ).wait_recv()
 
+    own_copy.wait()
     product = None
     for q in range(n_src):
         s = lax.rem(col // 2 + q, n_src)
@@ -323,7 +321,6 @@
         in_specs=[in_hbm, in_hbm, in_hbm, pl.BlockSpec(memory_space=pltpu.SMEM), in_hbm],
         out_specs=pl.BlockSpec(memory_space=pltpu.VMEM),
         scratch_shapes=[
-            pltpu.VMEM((2, rows, half), BF16),
             pltpu.VMEM((n_col * rows, half), BF16),
             pltpu.VMEM((2, slots, tile, tile), BF16),
             pltpu.VMEM(weight.shape, BF16),
@@ -333,7 +330,7 @@
             pltpu.VMEM((2 * targets, half), F32),
             pltpu.VMEM((2, n_row, rows, half), BF16),
             pltpu.VMEM((2, n_row, rows, half), BF16),
-            dma, dma((3,)), dma, dma,
+            dma, dma, dma, dma,
             dma((2,)), dma((2,)),
             dma((n_col,)), dma((n_col,)),
             dma((2, n_row)), dma((2, n_row)),

time: 17.8 us -> 17.8 us (level)
  no operation moved by 1% of the time
where the time goes in v6:
time: 17.8 us; the launch traced here: 17.6 us
  Pallas kernels  16.4 us (92%)
  between operations  0.66 us (4%)
  local copies, waits for them, and re-layouts  0.62 us (3%)
    pallas_call x1, Pallas kernels, pair_call(): pl.pallas_call(functools.partial(pair_kernel, n_row, n_col), out_shape=ja...  16.4 us
    unnamed x1, local copies, waits for them, and re-layouts  0.62 us

profile of v6, /device:TPU:0, one launch (start us, length us, event | category | flops | bytes accessed | tf_op | source)
XLA Modules:
  0.0 17.6 jit_solution(1272879512464344926)
XLA Ops:
  0.7 16.4 %shard_map.55 = bf16[64,256]{1,0:T(8,128)(2,1)S(1)} custom-call(bf16[64,256]{1,0:T(8,128)(2,1)} %x_ref.1, bf16[1,1,3,128,128]{4,3,2,1,0:T(8,128)(2,1)} %adj_ref.1, s32[1,1,3]{2,1,0:T(1,128)} %coord_ref.1, s32[1,1]{1,0:T(1,128)S(6)} %copy.7.count_ref, bf16[256,256]{1,0:T(8,128)(2,1)} %w_ref.1), custom_call_target="tpu_custom_call" | custom-call | tf_op jit(solution)/shard_map/pallas_call | solution.py:318
  17.0 0.6 %copy.8 = bf16[64,256]{1,0:T(8,128)(2,1)} copy(bf16[64,256]{1,0:T(8,128)(2,1)S(1)} %shard_map.55) | data formatting | bytes 65536

commit v7 on v5

--- a/solution.py
+++ b/solution.py
@@ -261,19 +261,6 @@
             recv_sem=col_recv.at[c], device_id={"col": pair}, device_id_type=MESH,
         ).wait_recv()
 
-    product = None
-    for q in range(n_src):
-        s = lax.rem(col // 2 + q, n_src)
-        if q == 0:
-            arrived(pair)
-        else:
-            arrived(2 * s)
-            arrived(2 * s + 1)
-        values = feats[pl.ds(pl.multiple_of(s * tile, tile), tile), :]
-        term = jnp.dot(dense[s], values, preferred_element_type=F32)
-        product = term if q == 0 else product + term
-    total[...] = product
-
     def row_copy(e, d):
         return pltpu.make_async_remote_copy(
             src_ref=stage.at[e, d], dst_ref=parts.at[e, d], send_sem=row_send.at[e, d],
@@ -283,9 +270,24 @@
     def block_of(e, r):
         return total[pl.ds(pl.multiple_of(e * targets + r * rows, rows), rows), :]
 
-    for e, d in row_peers:
-        stage[e, d] = block_of(e, lax.rem(row + d, n_row)).astype(stage.dtype)
-        row_copy(e, d).start()
+    for side_of in (1, 0):
+        product = None
+        for q in range(n_src):
+            s = lax.rem(col // 2 + q, n_src)
+            if side_of == 1 and q == 0:
+                arrived(pair)
+            elif side_of == 1:
+                arrived(2 * s)
+                arrived(2 * s + 1)
+            values = feats[pl.ds(pl.multiple_of(s * tile, tile), tile), :]
+            tiles = dense[s, pl.ds(side_of * targets, targets), :]
+            term = jnp.dot(tiles, values, preferred_element_type=F32)
+            product = term if q == 0 else product + term
+        total[pl.ds(side_of * targets, targets), :] = product
+        for e, d in row_peers:
+            if e == side_of:
+                stage[e, d] = block_of(e, lax.rem(row + d, n_row)).astype(stage.dtype)
+                row_copy(e, d).start()
     weight_copy.wait()
     hidden = [block_of(0, row), jnp.zeros((rows, half), F32)]
     for e, d in reversed(row_peers):

time: 17.8 us -> 17.5 us (0.983)
  Pallas kernels: 16.4 us -> 16 us
    pallas_call x1, Pallas kernels: 16.4 us -> 16 us  [pair_call(): pl.pallas_call(functools.partial(pair_kernel, n_row, n_col), out_shape=ja...]
where the time goes in v7:
time: 17.5 us; the launch traced here: 17.3 us
  Pallas kernels  16 us (91%)
  between operations  0.66 us (4%)
  local copies, waits for them, and re-layouts  0.62 us (4%)
    pallas_call x1, Pallas kernels, pair_call(): pl.pallas_call(functools.partial(pair_kernel, n_row, n_col), out_shape=ja...  16 us
    unnamed x1, local copies, waits for them, and re-layouts  0.62 us

profile of v7, /device:TPU:0, one launch (start us, length us, event | category | flops | bytes accessed | tf_op | source)
XLA Modules:
  0.0 17.3 jit_solution(12012931089873576565)
XLA Ops:
  0.7 16.0 %shard_map.55 = bf16[64,256]{1,0:T(8,128)(2,1)S(1)} custom-call(bf16[64,256]{1,0:T(8,128)(2,1)} %x_ref.1, bf16[1,1,3,128,128]{4,3,2,1,0:T(8,128)(2,1)} %adj_ref.1, s32[1,1,3]{2,1,0:T(1,128)} %coord_ref.1, s32[1,1]{1,0:T(1,128)S(6)} %copy.7.count_ref, bf16[256,256]{1,0:T(8,128)(2,1)} %w_ref.1), custom_call_target="tpu_custom_call" | custom-call | tf_op jit(solution)/shard_map/pallas_call | solution.py:322
  16.7 0.6 %copy.8 = bf16[64,256]{1,0:T(8,128)(2,1)} copy(bf16[64,256]{1,0:T(8,128)(2,1)S(1)} %shard_map.55) | data formatting | bytes 65536
